TPU v7x, 32 devices: a whole 2x2x4 slice. The times are simulated.
32 devices in a mesh: grp: 1, outer: 32 (over z, y, x, core).
Axes of the slice: x: 2, y: 2, z: 4, core: 2. Of those that a mesh axis runs over, the one named last changes fastest.
Arguments:
- grad_out: bfloat16 [1024, 512, 128], P(('grp', 'outer')), may hold values from -6 to 6
- input_spec: bfloat16 [2, 1024, 512, 128], P(None, ('grp', 'outer')), may hold values from -6 to 6
- kernel_spec: bfloat16 [2, 1024, 512, 128], P(None, 'outer'), may hold values from -6 to 6
- filter_hidden: bfloat16 [1024, 512, 64], P('outer'), may hold values from -6 to 6
- filter_w: bfloat16 [64, 128], replicated, may hold values from -0.75 to 0.75
- decay: float32 [128], replicated, may hold values from 0.3 to 30
Outputs:
- grad_input: bfloat16 [1024, 512, 128], P(('grp', 'outer'))
- grad_filter_w: float32 [64, 128], P('grp')
- grad_decay: float32 [128], P('grp')
All inputs are finite; a program needn't handle non-finite values.
Results may differ from a plain program's by a relative error of at most 0.0091.
Values may be sent and summed in bfloat16 or wider, within the bound.
A program may use at most 192 MiB of HBM per device.

v0:
```python
import math

import jax
import jax.numpy as jnp
from jax import lax
from jax.sharding import PartitionSpec as P


def cos_sin(length):
    numbers = jnp.arange(length, dtype=jnp.int32)
    product = numbers[:, None] * numbers[None, :] % length
    angles = product.astype(jnp.float32) * (2.0 * math.pi / length)
    return (jnp.cos(angles).astype(jnp.bfloat16), jnp.sin(angles).astype(jnp.bfloat16))


def twiddle(freq_numbers, time_numbers, seq_len):
    product = freq_numbers[:, None] * time_numbers[None, :] % seq_len
    angles = product.astype(jnp.float32) * (2.0 * math.pi / seq_len)
    return (jnp.cos(angles)[:, :, None], jnp.sin(angles)[:, :, None])


def outer_section(matrix, values):
    full_shape = values.shape
    flattened = values.reshape(full_shape[0], -1)
    return jnp.dot(matrix, flattened, preferred_element_type=jnp.float32).reshape(full_shape)


def inner_section(values, matrix):
    return jnp.einsum("cbh,bd->cdh", values, matrix, preferred_element_type=jnp.float32)


def shards(grad_out, input_spec, kernel_spec, filter_hidden, filter_w, decay):
    devices = lax.axis_size("outer")
    my_index = lax.axis_index("outer")
    rows_dev = grad_out.shape[0]
    inner_len = grad_out.shape[1]
    outer_len = rows_dev * devices
    seq_len = outer_len * inner_len
    cols_dev = inner_len // devices
    freq_dev = input_spec.shape[1]
    inv_total = 1.0 / seq_len
    inv_root = 1.0 / math.sqrt(seq_len)
    cosine_outer, sine_outer = cos_sin(outer_len)
    cosine_inner, sine_inner = cos_sin(inner_len)
    my_rows = my_index * rows_dev + jnp.arange(rows_dev, dtype=jnp.int32)
    row_positions = (
        my_rows[:, None] * inner_len + jnp.arange(inner_len, dtype=jnp.int32)[None, :]
    ).astype(jnp.float32) * inv_total
    columns = lax.all_to_all(grad_out, "outer", split_axis=1, concat_axis=0, tiled=True)
    part_real = outer_section(cosine_outer, columns)
    part_imag = -outer_section(sine_outer, columns)
    my_cols = my_index * cols_dev + jnp.arange(cols_dev, dtype=jnp.int32)
    twist_cos, twist_sin = twiddle(jnp.arange(outer_len, dtype=jnp.int32), my_cols, seq_len)
    shifted_real = (part_real * twist_cos + part_imag * twist_sin).astype(jnp.bfloat16)
    shifted_imag = (part_imag * twist_cos - part_real * twist_sin).astype(jnp.bfloat16)
    freq_real, freq_imag = (
        lax.all_to_all(shifted_real, "outer", split_axis=0, concat_axis=1, tiled=True),
        lax.all_to_all(shifted_imag, "outer", split_axis=0, concat_axis=1, tiled=True),
    )
    spec_real = inner_section(freq_real, cosine_inner) + inner_section(freq_imag, sine_inner)
    spec_imag = inner_section(freq_imag, cosine_inner) - inner_section(freq_real, sine_inner)
    my_freq = my_index * freq_dev + jnp.arange(freq_dev, dtype=jnp.int32)
    back_cos, back_sin = twiddle(my_freq, jnp.arange(inner_len, dtype=jnp.int32), seq_len)

    def correlate(spectrum):
        real_part = spectrum[0].astype(jnp.float32)
        imag_part = spectrum[1].astype(jnp.float32)
        return (
            (real_part * spec_real + imag_part * spec_imag).astype(jnp.bfloat16),
            (real_part * spec_imag - imag_part * spec_real).astype(jnp.bfloat16),
        )

    def inverse_inner(halves):
        real_part, imag_part = halves
        mixed_real = inner_section(real_part, cosine_inner) - inner_section(imag_part, sine_inner)
        mixed_imag = inner_section(imag_part, cosine_inner) + inner_section(real_part, sine_inner)
        return (
            (mixed_real * back_cos - mixed_imag * back_sin).astype(jnp.bfloat16),
            (mixed_imag * back_cos + mixed_real * back_sin).astype(jnp.bfloat16),
        )

    def last_section(real_part, imag_part):
        summed = outer_section(cosine_outer, real_part) - outer_section(sine_outer, imag_part)
        return (summed * inv_total).astype(jnp.bfloat16)

    def one_last(halves):
        return last_section(halves[0], halves[1])

    input_turned = inverse_inner(correlate(kernel_spec))
    grad_cols = one_last(
        (
            lax.all_to_all(input_turned[0], "outer", split_axis=1, concat_axis=0, tiled=True),
            lax.all_to_all(input_turned[1], "outer", split_axis=1, concat_axis=0, tiled=True),
        )
    )
    kernel_turned = inverse_inner(correlate(input_spec))
    kern_cols = one_last(
        (
            lax.all_to_all(kernel_turned[0], "outer", split_axis=1, concat_axis=0, tiled=True),
            lax.all_to_all(kernel_turned[1], "outer", split_axis=1, concat_axis=0, tiled=True),
        )
    )
    grad_rows, kern_here = (
        lax.all_to_all(grad_cols, "outer", split_axis=0, concat_axis=1, tiled=True),
        lax.all_to_all(kern_cols, "outer", split_axis=0, concat_axis=1, tiled=True),
    )
    kernel_values = kern_here.astype(jnp.float32)
    window = jnp.exp(-decay * row_positions[:, :, None])
    raw_filter = jnp.einsum(
        "abf,fh->abh", filter_hidden, filter_w, preferred_element_type=jnp.float32
    )
    scaled = (kernel_values * window * inv_root).astype(jnp.bfloat16)
    weight_part = jnp.einsum(
        "abf,abh->fh", filter_hidden, scaled, preferred_element_type=jnp.float32
    )
    decay_part = (
        -jnp.sum(row_positions[:, :, None] * window * raw_filter * kernel_values, axis=(0, 1))
        * inv_root
    )
    grad_filter_w, grad_decay = lax.psum((weight_part, decay_part), "outer")
    return (grad_rows, grad_filter_w, grad_decay)


def solution(mesh):
    placed = (
        P(("grp", "outer"), None, None),
        P(None, ("grp", "outer"), None, None),
        P(None, "outer", None, None),
        P("outer", None, None),
        P(),
        P(),
    )
    return jax.shard_map(
        shards,
        mesh=mesh,
        in_specs=placed,
        out_specs=(P(("grp", "outer"), None, None), P("grp", None), P("grp")),
        check_vma=False,
    )
```

profile of v0, /device:TPU:0, one launch (start us, length us, event | category | flops | bytes accessed | tf_op | source)
XLA Modules:
  0.0 1132.7 jit_solution(8463302655406066317)
XLA Ops:
  0.6 7.0 copy.28
  7.7 7.4 all-to-all-start
  15.5 93.5 %all-to-all-done = bf16[32,512,128]{2,0,1:T(8,128)(2,1)} async-done(((bf16[32,512,128]{2,0,1:T(8,128)(2,1)}), bf16[32,512,128]{2,0,1:T(8,128)(2,1)}, u32[]{:S(2)}, u32[]{:S(2)}) %all-to-all-start) | async-done | bytes 4194336 | tf_op jit(solution)/shard_map/all_to_all | solution.py:49
  109.0 4.2 copy.29
  113.2 4.1 copy.65
  117.3 6.6 copy.30
  123.9 34.0 %fusion.29 = f32[1024,16,128]{2,0,1:T(8,128)S(1)} fusion(bf16[16,128,1024]{2,1,0:T(8,128)(2,1)} %bitcast.219), kind=kOutput, calls=%fused_computation.62 | convolution fusion | flops 4310695936 | bytes 12582912 | tf_op jit(solution)/shard_map/dot_general | solution.py:25
  157.9 23.7 %add_convert_fusion = (bf16[1024,16,128]{2,0,1:T(8,128)(2,1)S(1)}, bf16[1024,16,128]{2,0,1:T(8,128)(2,1)}) fusion(f32[1024,16,128]{2,0,1:T(8,128)S(1)} %fusion.29, f32[1024,16]{0,1:T(8,128)S(1)} %get-tuple-element.20, f32[1024,16]{0,1:T(8,128)S(1)} %get-tuple-element.19, bf16[16,128,1024]{2,1,0:T(8,128)(2,1)S(1)} %bitcast.220), kind=kOutput, calls=%fused_computation.41 | convolution fusion | flops 4329570304 | bytes 21102592 | tf_op jit(solution)/shard_map/dot_general | solution.py:25
  181.7 4.7 copy.31
  186.4 4.1 all-to-all-start.1
  190.5 6.8 copy.33
  197.3 87.0 %all-to-all-done.1 = bf16[1024,16,128]{2,1,0:T(8,128)(2,1)} async-done(((bf16[1024,16,128]{2,1,0:T(8,128)(2,1)}), bf16[1024,16,128]{2,1,0:T(8,128)(2,1)}, u32[]{:S(2)}, u32[]{:S(2)}) %all-to-all-start.1) | async-done | bytes 4194336 | tf_op jit(solution)/shard_map/all_to_all | solution.py:57
  284.3 4.5 all-to-all-start.2
  289.2 3.4 copy.32
  294.6 8.0 fusion.65
  302.6 80.2 %all-to-all-done.2 = bf16[1024,16,128]{2,1,0:T(8,128)(2,1)} async-done(((bf16[1024,16,128]{2,1,0:T(8,128)(2,1)}), bf16[1024,16,128]{2,1,0:T(8,128)(2,1)}, u32[]{:S(2)}, u32[]{:S(2)}) %all-to-all-start.2) | async-done | bytes 4194336 | tf_op jit(solution)/shard_map/all_to_all | solution.py:58
  386.2 8.0 fusion.63
  394.2 8.1 convolution_add_fusion
  402.3 19.4 %fusion.5 = (bf16[32,512,128]{2,1,0:T(8,128)(2,1)S(1)}, bf16[32,512,128]{2,1,0:T(8,128)(2,1)}, bf16[32,512,128]{2,1,0:T(8,128)(2,1)}, bf16[32,512,128]{2,1,0:T(8,128)(2,1)}) fusion(f32[512,32,128]{2,0,1:T(8,128)} %convolution_add_fusion, bf16[2,32,512,128]{3,2,1,0:T(8,128)(2,1)} %param.7, bf16[2,32,512,128]{3,2,1,0:T(8,128)(2,1)} %param.8, ...), kind=kOutput, calls=%fused_computation.13 | convolution fusion | flops 2195456000 | bytes 54525952 | tf_op jit(solution)/shard_map/cbh,bd->cdh/dot_general | solution.py:29
  421.6 5.9 fusion.45
  427.6 5.9 fusion.57
  433.5 6.2 fusion.51
  439.7 8.0 fusion.59
  447.7 8.0 fusion.49
  455.7 8.0 fusion.61
  463.7 8.4 fusion.47
  472.1 21.1 %fusion.14 = (bf16[32,512,128]{2,1,0:T(8,128)(2,1)}, bf16[32,512,128]{2,1,0:T(8,128)(2,1)}, bf16[32,512,128]{2,1,0:T(8,128)(2,1)}, bf16[32,512,128]{2,1,0:T(8,128)(2,1)}) fusion(f32[32,512]{1,0:T(8,128)S(1)} %get-tuple-element.22, f32[32,512]{1,0:T(8,128)S(1)} %get-tuple-element.21, f32[512,32,128]{2,0,1:T(8,128)S(1)} %fusion.45, ...), kind=kOutput, calls=%fused_computation.26 | convolution fusion | flops 2193358848 | bytes 79822848 | tf_op jit(solution)/shard_map/cbh,bd->cdh/dot_general | solution.py:29
  493.2 6.9 copy.43
  500.1 4.0 all-to-all-start.6
  504.2 6.8 copy.46
  511.0 87.0 %all-to-all-done.6 = bf16[32,512,128]{2,0,1:T(8,128)(2,1)} async-done(((bf16[32,512,128]{2,0,1:T(8,128)(2,1)}), bf16[32,512,128]{2,0,1:T(8,128)(2,1)}, u32[]{:S(2)}, u32[]{:S(2)}) %all-to-all-start.6) | async-done | bytes 4194336 | tf_op jit(solution)/shard_map/all_to_all | solution.py:99
  598.1 4.3 all-to-all-start.7
  602.3 6.9 copy.35
  609.2 87.0 %all-to-all-done.7 = bf16[32,512,128]{2,0,1:T(8,128)(2,1)} async-done(((bf16[32,512,128]{2,0,1:T(8,128)(2,1)}), bf16[32,512,128]{2,0,1:T(8,128)(2,1)}, u32[]{:S(2)}, u32[]{:S(2)}) %all-to-all-start.7) | async-done | bytes 4194336 | tf_op jit(solution)/shard_map/all_to_all | solution.py:100
  696.2 4.0 all-to-all-start.3
  700.3 6.8 copy.38
  707.1 87.0 %all-to-all-done.3 = bf16[32,512,128]{2,0,1:T(8,128)(2,1)} async-done(((bf16[32,512,128]{2,0,1:T(8,128)(2,1)}), bf16[32,512,128]{2,0,1:T(8,128)(2,1)}, u32[]{:S(2)}, u32[]{:S(2)}) %all-to-all-start.3) | async-done | bytes 4194336 | tf_op jit(solution)/shard_map/all_to_all | solution.py:92
  794.2 4.3 all-to-all-start.4
  798.5 4.2 copy.44
  802.6 4.1 copy.62
  806.8 6.4 copy.45
  813.2 4.2 copy.47
  817.3 4.1 copy.61
  821.5 6.8 copy.48
  828.2 21.3 %fusion.31 = f32[1024,16,128]{2,0,1:T(8,128)S(1)} fusion(bf16[16,128,1024]{2,1,0:T(8,128)(2,1)} %bitcast.221), kind=kOutput, calls=%fused_computation.63 | convolution fusion | flops 4310695936 | bytes 12582912 | tf_op jit(solution)/shard_map/dot_general | solution.py:25
  849.6 20.1 %multiply_convert_fusion = bf16[1024,16,128]{2,0,1:T(8,128)(2,1)S(1)} fusion(f32[1024,16,128]{2,0,1:T(8,128)S(1)} %fusion.31, bf16[16,128,1024]{2,1,0:T(8,128)(2,1)S(1)} %bitcast.223), kind=kOutput, calls=%fused_computation.38 | convolution fusion | flops 4316987392 | bytes 16777216 | tf_op jit(solution)/shard_map/dot_general | solution.py:25
  869.7 4.7 copy.49
  874.4 18.0 %all-to-all-done.4 = bf16[32,512,128]{2,0,1:T(8,128)(2,1)} async-done(((bf16[32,512,128]{2,0,1:T(8,128)(2,1)}), bf16[32,512,128]{2,0,1:T(8,128)(2,1)}, u32[]{:S(2)}, u32[]{:S(2)}) %all-to-all-start.4) | async-done | bytes 4194336 | tf_op jit(solution)/shard_map/all_to_all | solution.py:93
  892.4 4.0 all-to-all-start.8
  896.5 4.2 copy.36
  900.6 4.1 copy.64
  904.7 6.4 copy.37
  911.1 4.2 copy.39
  915.3 4.1 copy.63
  919.4 6.9 copy.40
  926.3 21.4 %fusion.33 = f32[1024,16,128]{2,0,1:T(8,128)S(1)} fusion(bf16[16,128,1024]{2,1,0:T(8,128)(2,1)} %bitcast.222), kind=kOutput, calls=%fused_computation.64 | convolution fusion | flops 4310695936 | bytes 12582912 | tf_op jit(solution)/shard_map/dot_general | solution.py:25
  947.7 20.1 %multiply_convert_fusion.1 = bf16[1024,16,128]{2,0,1:T(8,128)(2,1)S(1)} fusion(f32[1024,16,128]{2,0,1:T(8,128)S(1)} %fusion.33, bf16[16,128,1024]{2,1,0:T(8,128)(2,1)S(1)} %bitcast.224), kind=kOutput, calls=%fused_computation.39 | convolution fusion | flops 4316987392 | bytes 16777216 | tf_op jit(solution)/shard_map/dot_general | solution.py:25
  967.8 4.7 copy.41
  972.5 17.8 %all-to-all-done.8 = bf16[1024,16,128]{2,1,0:T(8,128)(2,1)} async-done(((bf16[1024,16,128]{2,1,0:T(8,128)(2,1)}), bf16[1024,16,128]{2,1,0:T(8,128)(2,1)}, u32[]{:S(2)}, u32[]{:S(2)}) %all-to-all-start.8) | async-done | bytes 4194336 | tf_op jit(solution)/shard_map/all_to_all | solution.py:105
  990.3 4.1 all-to-all-start.5
  997.8 4.3 fusion.10
  1006.2 82.1 %all-to-all-done.5 = bf16[1024,16,128]{2,1,0:T(8,128)(2,1)} async-done(((bf16[1024,16,128]{2,1,0:T(8,128)(2,1)}), bf16[1024,16,128]{2,1,0:T(8,128)(2,1)}, u32[]{:S(2)}, u32[]{:S(2)}) %all-to-all-start.5) | async-done | bytes 4194336 | tf_op jit(solution)/shard_map/all_to_all | solution.py:104
  1088.3 5.4 copy.42
  1093.7 38.8 %all-reduce = (f32[64,128]{1,0:T(8,128)}, f32[128]{0:T(128)}) all-reduce(f32[64,128]{1,0:T(8,128)S(1)} %convolution_bitcast_fusion, f32[128]{0:T(128)S(1)} %negate_multiply_fusion), channel_id=1, replica_groups=mesh['grp'=1,'outer'=32] {'outer'}, use_global_device_ids=true, to_apply=%region_0.1 | all-reduce | flops 8320 | bytes 66560 | tf_op jit(solution)/shard_map/psum | solution.py:120
  (39 shorter events, 13.4 us)
Async XLA Ops:
  0.6 997.2 %copy-start = (bf16[32,512,64]{1,2,0:T(8,128)(2,1)S(1)}, bf16[32,512,64]{1,2,0:T(8,128)(2,1)}, u32[]{:S(2)}) copy-start(bf16[32,512,64]{1,2,0:T(8,128)(2,1)} %param.9) | copy-start | bytes 6291460
  7.7 101.3 %all-to-all-start = ((bf16[32,512,128]{2,0,1:T(8,128)(2,1)}), bf16[32,512,128]{2,0,1:T(8,128)(2,1)}, u32[]{:S(2)}, u32[]{:S(2)}) async-start(bf16[32,512,128]{2,0,1:T(8,128)(2,1)} %copy.28), calls=%async_computation | async-start | bytes 8388608 | tf_op jit(solution)/shard_map/all_to_all | solution.py:49
  123.9 34.0 %copy-start.6 = (bf16[2048,1024]{1,0:T(8,128)(2,1)S(1)}, bf16[2048,1024]{1,0:T(8,128)(2,1)}, u32[]{:S(2)}) copy-start(bf16[2048,1024]{1,0:T(8,128)(2,1)} %copy.30) | copy-start | bytes 12582916
  186.4 98.0 %all-to-all-start.1 = ((bf16[1024,16,128]{2,1,0:T(8,128)(2,1)}), bf16[1024,16,128]{2,1,0:T(8,128)(2,1)}, u32[]{:S(2)}, u32[]{:S(2)}) async-start(bf16[1024,16,128]{2,1,0:T(8,128)(2,1)} %copy.31), calls=%async_computation.1 | async-start | bytes 8388608 | tf_op jit(solution)/shard_map/all_to_all | solution.py:57
  284.3 98.4 %all-to-all-start.2 = ((bf16[1024,16,128]{2,1,0:T(8,128)(2,1)}), bf16[1024,16,128]{2,1,0:T(8,128)(2,1)}, u32[]{:S(2)}, u32[]{:S(2)}) async-start(bf16[1024,16,128]{2,1,0:T(8,128)(2,1)} %copy.33), calls=%async_computation.2 | async-start | bytes 8388608 | tf_op jit(solution)/shard_map/all_to_all | solution.py:58
  292.6 2.0 copy-start.4
  386.1 8.0 slice-start
  386.1 8.0 slice-start.1
  394.2 8.1 copy-start.5
  427.6 5.9 copy-start.2
  439.7 8.0 copy-start.1
  455.7 8.0 copy-start.3
  500.1 97.9 %all-to-all-start.6 = ((bf16[32,512,128]{2,0,1:T(8,128)(2,1)}), bf16[32,512,128]{2,0,1:T(8,128)(2,1)}, u32[]{:S(2)}, u32[]{:S(2)}) async-start(bf16[32,512,128]{2,0,1:T(8,128)(2,1)} %copy.43), calls=%async_computation.6 | async-start | bytes 8388608 | tf_op jit(solution)/shard_map/all_to_all | solution.py:99
  598.1 98.2 %all-to-all-start.7 = ((bf16[32,512,128]{2,0,1:T(8,128)(2,1)}), bf16[32,512,128]{2,0,1:T(8,128)(2,1)}, u32[]{:S(2)}, u32[]{:S(2)}) async-start(bf16[32,512,128]{2,0,1:T(8,128)(2,1)} %copy.46), calls=%async_computation.7 | async-start | bytes 8388608 | tf_op jit(solution)/shard_map/all_to_all | solution.py:100
  696.2 97.9 %all-to-all-start.3 = ((bf16[32,512,128]{2,0,1:T(8,128)(2,1)}), bf16[32,512,128]{2,0,1:T(8,128)(2,1)}, u32[]{:S(2)}, u32[]{:S(2)}) async-start(bf16[32,512,128]{2,0,1:T(8,128)(2,1)} %copy.35), calls=%async_computation.3 | async-start | bytes 8388608 | tf_op jit(solution)/shard_map/all_to_all | solution.py:92
  794.2 98.2 %all-to-all-start.4 = ((bf16[32,512,128]{2,0,1:T(8,128)(2,1)}), bf16[32,512,128]{2,0,1:T(8,128)(2,1)}, u32[]{:S(2)}, u32[]{:S(2)}) async-start(bf16[32,512,128]{2,0,1:T(8,128)(2,1)} %copy.38), calls=%async_computation.4 | async-start | bytes 8388608 | tf_op jit(solution)/shard_map/all_to_all | solution.py:93
  828.2 21.4 %copy-start.7 = (bf16[2048,1024]{1,0:T(8,128)(2,1)S(1)}, bf16[2048,1024]{1,0:T(8,128)(2,1)}, u32[]{:S(2)}) copy-start(bf16[2048,1024]{1,0:T(8,128)(2,1)} %copy.48) | copy-start | bytes 12582916
  892.4 97.9 %all-to-all-start.8 = ((bf16[1024,16,128]{2,1,0:T(8,128)(2,1)}), bf16[1024,16,128]{2,1,0:T(8,128)(2,1)}, u32[]{:S(2)}, u32[]{:S(2)}) async-start(bf16[1024,16,128]{2,1,0:T(8,128)(2,1)} %copy.49), calls=%async_computation.8 | async-start | bytes 8388608 | tf_op jit(solution)/shard_map/all_to_all | solution.py:105
  926.3 21.4 %copy-start.8 = (bf16[2048,1024]{1,0:T(8,128)(2,1)S(1)}, bf16[2048,1024]{1,0:T(8,128)(2,1)}, u32[]{:S(2)}) copy-start(bf16[2048,1024]{1,0:T(8,128)(2,1)} %copy.40) | copy-start | bytes 12582916
  972.5 21.9 %copy-start.10 = (f32[128]{0:T(128)S(1)}, f32[128]{0:T(128)}, u32[]{:S(2)}) copy-start(f32[128]{0:T(128)} %param.11) | copy-start | bytes 1540
  990.3 98.0 %all-to-all-start.5 = ((bf16[1024,16,128]{2,1,0:T(8,128)(2,1)}), bf16[1024,16,128]{2,1,0:T(8,128)(2,1)}, u32[]{:S(2)}, u32[]{:S(2)}) async-start(bf16[1024,16,128]{2,1,0:T(8,128)(2,1)} %copy.41), calls=%async_computation.5 | async-start | bytes 8388608 | tf_op jit(solution)/shard_map/all_to_all | solution.py:104
  994.6 3.2 copy-start.9
where the time goes:
time: 1130 us
  waiting for transfers between devices  640 us (57%)
  matrix products  261 us (23%)
  local copies, waits for them, and re-layouts  147 us (13%)
  starting transfers between devices  40.8 us (4%)
  blocking collectives  38.8 us (3%)
    dot_general x6, matrix products, outer_section(): jnp.dot(matrix, flattened, preferred_element_type=jnp.float32)  141 us
    dot_general x12, matrix products, inner_section(): jnp.einsum('cbh,bd->cdh', values, matrix, preferred_element_type=jnp.floa...  115 us
    all_to_all x1, waiting for transfers between devices, shards(): lax.all_to_all(grad_out, 'outer', split_axis=1, concat_axis=0, tiled=True)  93.5 us
    all_to_all x1, waiting for transfers between devices, shards(): lax.all_to_all(kernel_turned[0], 'outer', split_axis=1, concat_axis=0, ti...  87 us
    all_to_all x1, waiting for transfers between devices, shards(): lax.all_to_all(input_turned[0], 'outer', split_axis=1, concat_axis=0, til...  87 us
    all_to_all x1, waiting for transfers between devices, shards(): lax.all_to_all(shifted_real, 'outer', split_axis=0, concat_axis=1, tiled=...  87 us
    all_to_all x1, waiting for transfers between devices, shards(): lax.all_to_all(kernel_turned[1], 'outer', split_axis=1, concat_axis=0, ti...  87 us
    all_to_all x1, waiting for transfers between devices, shards(): lax.all_to_all(grad_cols, 'outer', split_axis=0, concat_axis=1, tiled=True)  82.1 us
  transfers between devices with their start and end apart: 9, of which 9 were waited for; matrix products, arithmetic and copies ran while one was open for 18% of the time, Pallas kernels for 0%

commit v1 on v0

--- a/solution.py
+++ b/solution.py
@@ -1,9 +1,16 @@
+import functools
 import math
 
 import jax
 import jax.numpy as jnp
 from jax import lax
+from jax.experimental import pallas as pl
+from jax.experimental.pallas import tpu as pltpu
 from jax.sharding import PartitionSpec as P
+
+VMEM_BYTES = 56 * 1024 * 1024
+PAIR = 2
+ROWS = 4
 
 
 def cos_sin(length):
@@ -29,7 +36,7 @@
     return jnp.einsum("cbh,bd->cdh", values, matrix, preferred_element_type=jnp.float32)
 
 
-def shards(grad_out, input_spec, kernel_spec, filter_hidden, filter_w, decay):
+def plain_shards(grad_out, input_spec, kernel_spec, filter_hidden, filter_w, decay):
     devices = lax.axis_size("outer")
     my_index = lax.axis_index("outer")
     rows_dev = grad_out.shape[0]
@@ -121,6 +128,273 @@
     return (grad_rows, grad_filter_w, grad_decay)
 
 
+def dot(matrix, values):
+    return jnp.dot(matrix, values, preferred_element_type=jnp.float32)
+
+
+def beside(blocks):
+    return jnp.concatenate(blocks, axis=1)
+
+
+def call(kernel, grid, in_specs, out_specs, out_shape, flops, moved, *operands):
+    return pl.pallas_call(
+        kernel,
+        grid=(grid,),
+        in_specs=in_specs,
+        out_specs=out_specs,
+        out_shape=out_shape,
+        compiler_params=pltpu.CompilerParams(
+            dimension_semantics=("arbitrary",), vmem_limit_bytes=VMEM_BYTES
+        ),
+        cost_estimate=pl.CostEstimate(flops=flops, bytes_accessed=moved, transcendentals=0),
+    )(*operands)
+
+
+def whole(array):
+    zeros = (0,) * array.ndim
+    return pl.BlockSpec(array.shape, lambda step: zeros)
+
+
+def block(array, axis, size):
+    shape = array.shape[:axis] + (size,) + array.shape[axis + 1 :]
+    return pl.BlockSpec(
+        shape, lambda step: tuple(step if at == axis else 0 for at in range(len(shape)))
+    )
+
+
+def outer_forward_kernel(cos_ref, sin_ref, tc_ref, ts_ref, x_ref, real_ref, imag_ref):
+    lanes = x_ref.shape[-1]
+    values = beside([x_ref[:, k].reshape(-1, lanes) for k in range(PAIR)])
+    real = dot(cos_ref[...], values)
+    imag = -dot(sin_ref[...], values)
+    for k in range(PAIR):
+        r = real[:, k * lanes : (k + 1) * lanes]
+        i = imag[:, k * lanes : (k + 1) * lanes]
+        real_ref[k] = (r * tc_ref[k] + i * ts_ref[k]).astype(jnp.bfloat16)
+        imag_ref[k] = (i * tc_ref[k] - r * ts_ref[k]).astype(jnp.bfloat16)
+
+
+def inner_kernel(cos_ref, sin_ref, tc_ref, ts_ref, fr_ref, fi_ref, s_ref, real_ref, imag_ref):
+    lanes = fr_ref.shape[-1]
+    cosine, sine = cos_ref[...], sin_ref[...]
+    in_real = beside([fr_ref[:, k].reshape(-1, lanes) for k in range(ROWS)])
+    in_imag = beside([fi_ref[:, k].reshape(-1, lanes) for k in range(ROWS)])
+    spec_real = dot(cosine, in_real) + dot(sine, in_imag)
+    spec_imag = dot(cosine, in_imag) - dot(sine, in_real)
+    kept_real = beside([s_ref[0, k] for k in range(ROWS)]).astype(jnp.float32)
+    kept_imag = beside([s_ref[1, k] for k in range(ROWS)]).astype(jnp.float32)
+    corr_real = (kept_real * spec_real + kept_imag * spec_imag).astype(jnp.bfloat16)
+    corr_imag = (kept_real * spec_imag - kept_imag * spec_real).astype(jnp.bfloat16)
+    mixed_real = dot(cosine, corr_real) - dot(sine, corr_imag)
+    mixed_imag = dot(cosine, corr_imag) + dot(sine, corr_real)
+    out_shape = (real_ref.shape[0],) + real_ref.shape[2:]
+    for k in range(ROWS):
+        r = mixed_real[:, k * lanes : (k + 1) * lanes]
+        i = mixed_imag[:, k * lanes : (k + 1) * lanes]
+        turned_real = (r * tc_ref[k] - i * ts_ref[k]).astype(jnp.bfloat16)
+        turned_imag = (i * tc_ref[k] + r * ts_ref[k]).astype(jnp.bfloat16)
+        real_ref[:, k] = turned_real.reshape(out_shape)
+        imag_ref[:, k] = turned_imag.reshape(out_shape)
+
+
+def outer_inverse_kernel(inv_total, cos_ref, sin_ref, tr_ref, ti_ref, out_ref):
+    lanes = tr_ref.shape[-1]
+    real = beside([tr_ref[k] for k in range(PAIR)])
+    imag = beside([ti_ref[k] for k in range(PAIR)])
+    summed = (dot(cos_ref[...], real) - dot(sin_ref[...], imag)) * inv_total
+    for k in range(PAIR):
+        out_ref[k] = summed[:, k * lanes : (k + 1) * lanes].astype(jnp.bfloat16)
+
+
+def filter_kernel(
+    inner_len,
+    inv_total,
+    inv_root,
+    first_ref,
+    cos_ref,
+    sin_ref,
+    tr_ref,
+    ti_ref,
+    hidden_ref,
+    w_ref,
+    decay_ref,
+    weight_ref,
+    slope_ref,
+):
+    step = pl.program_id(0)
+
+    @pl.when(step == 0)
+    def _():
+        weight_ref[...] = jnp.zeros_like(weight_ref)
+        slope_ref[...] = jnp.zeros_like(slope_ref)
+
+    lanes = tr_ref.shape[-1]
+    real = beside([tr_ref[k] for k in range(PAIR)])
+    imag = beside([ti_ref[k] for k in range(PAIR)])
+    values = (dot(cos_ref[...], real) - dot(sin_ref[...], imag)) * inv_total
+    shape = values.shape
+    hidden = hidden_ref[:, 0].reshape(shape[0], hidden_ref.shape[-1])
+    row = lax.broadcasted_iota(jnp.int32, shape, 0)
+    lane = lax.broadcasted_iota(jnp.int32, shape, 1)
+    column = first_ref[0] + PAIR * step + (lane >= lanes).astype(jnp.int32)
+    position = (row * inner_len + column).astype(jnp.float32) * inv_total
+    weighted = jnp.exp(-decay_ref[...] * position) * values
+    raw_filter = dot(hidden, w_ref[...])
+    slope = position * weighted * raw_filter
+    slope_ref[...] += jnp.sum(slope.reshape(-1, 8, shape[1]), axis=0)
+    scaled = (weighted * inv_root).astype(jnp.bfloat16)
+    weight_ref[...] += lax.dot_general(
+        hidden, scaled, (((0,), (0,)), ((), ())), preferred_element_type=jnp.float32
+    )
+
+
+def shards(grad_out, input_spec, kernel_spec, filter_hidden, filter_w, decay):
+    devices = lax.axis_size("outer")
+    my_index = lax.axis_index("outer")
+    rows_dev, inner_len, lanes = grad_out.shape
+    outer_len = rows_dev * devices
+    seq_len = outer_len * inner_len
+    cols_dev = inner_len // devices
+    if rows_dev % 16 or cols_dev % 16 or devices % 2 or devices & (devices - 1):
+        return plain_shards(
+            grad_out, input_spec, kernel_spec, filter_hidden, filter_w, decay
+        )
+    freq_dev = input_spec.shape[1]
+    half = devices // 2
+    half_cols = inner_len // half
+    half_len = freq_dev * half
+    order = filter_hidden.shape[-1]
+    inv_total = 1.0 / seq_len
+    inv_root = 1.0 / math.sqrt(seq_len)
+    groups = [list(range(half)), list(range(half, devices))]
+    bf16 = functools.partial(jax.ShapeDtypeStruct, dtype=jnp.bfloat16)
+    f32 = functools.partial(jax.ShapeDtypeStruct, dtype=jnp.float32)
+    cosine_outer, sine_outer = cos_sin(outer_len)
+    cosine_inner, sine_inner = cos_sin(inner_len)
+
+    def exchange(values, axis_index_groups=None):
+        return lax.all_to_all(
+            values,
+            "outer",
+            split_axis=0,
+            concat_axis=0,
+            axis_index_groups=axis_index_groups,
+            tiled=True,
+        )
+
+    columns = exchange(
+        grad_out.reshape(rows_dev, devices, cols_dev, lanes).transpose(1, 2, 0, 3)
+    )
+    hidden = filter_hidden.reshape(rows_dev, half, half_cols // PAIR, PAIR * order)
+    hidden = hidden.transpose(1, 2, 0, 3)
+    hidden = jnp.concatenate((hidden, hidden), axis=0)
+    hidden, columns = lax.optimization_barrier((hidden, columns))
+    hidden = exchange(hidden)
+
+    my_cols = my_index * cols_dev + jnp.arange(cols_dev, dtype=jnp.int32)
+    twist_cos, twist_sin = twiddle(my_cols, jnp.arange(outer_len, dtype=jnp.int32), seq_len)
+    table_bytes = 4 * outer_len * outer_len
+    column_bytes = 2 * outer_len * cols_dev * lanes
+    turn_bytes = 8 * 128 * outer_len * cols_dev
+    outer_flops = 4 * outer_len * outer_len * cols_dev * lanes
+    inner_flops = 16 * freq_dev * inner_len * inner_len * lanes
+    shape = (cols_dev, outer_len, lanes)
+    shifted = call(
+        outer_forward_kernel,
+        cols_dev // PAIR,
+        [whole(cosine_outer), whole(sine_outer), block(twist_cos, 0, PAIR),
+         block(twist_sin, 0, PAIR), block(columns, 1, PAIR)],
+        [block(bf16(shape), 0, PAIR)] * 2,
+        [bf16(shape)] * 2,
+        outer_flops,
+        table_bytes + 3 * column_bytes + turn_bytes,
+        cosine_outer, sine_outer, twist_cos, twist_sin, columns,
+    )
+    freq_real, freq_imag = [
+        exchange(part.reshape(cols_dev, devices, freq_dev, lanes).transpose(1, 2, 0, 3))
+        for part in shifted
+    ]
+    my_freq = my_index * freq_dev + jnp.arange(freq_dev, dtype=jnp.int32)
+    back_cos, back_sin = twiddle(my_freq, jnp.arange(inner_len, dtype=jnp.int32), seq_len)
+
+    def turned_of(spectrum, freq_real, freq_imag, pieces):
+        shape = (pieces, freq_dev, inner_len // pieces, lanes)
+        return call(
+            inner_kernel,
+            freq_dev // ROWS,
+            [whole(cosine_inner), whole(sine_inner), block(back_cos, 0, ROWS),
+             block(back_sin, 0, ROWS), block(freq_real, 1, ROWS), block(freq_imag, 1, ROWS),
+             block(spectrum, 1, ROWS)],
+            [block(bf16(shape), 1, ROWS)] * 2,
+            [bf16(shape)] * 2,
+            inner_flops,
+            6 * column_bytes + turn_bytes,
+            cosine_inner, sine_inner, back_cos, back_sin, freq_real, freq_imag, spectrum,
+        )
+
+    def by_column(part):
+        return part.transpose(2, 0, 1, 3).reshape(part.shape[2], -1, lanes)
+
+    input_turned = turned_of(kernel_spec, freq_real, freq_imag, devices)
+    (freq_real, freq_imag), input_turned = lax.optimization_barrier(
+        ((freq_real, freq_imag), input_turned)
+    )
+    kernel_turned = turned_of(input_spec, freq_real, freq_imag, half)
+    input_parts = [by_column(exchange(part)) for part in input_turned]
+    kernel_parts = [exchange(part, groups) for part in kernel_turned]
+
+    grad_cols = call(
+        functools.partial(outer_inverse_kernel, inv_total),
+        cols_dev // PAIR,
+        [whole(cosine_outer), whole(sine_outer)] + [block(input_parts[0], 0, PAIR)] * 2,
+        block(bf16(shape), 0, PAIR),
+        bf16(shape),
+        outer_flops,
+        table_bytes + 3 * column_bytes,
+        cosine_outer, sine_outer, *input_parts,
+    )
+    grad_cols = grad_cols.reshape(cols_dev, devices, rows_dev, lanes).transpose(1, 2, 0, 3)
+    kernel_parts, grad_cols = lax.optimization_barrier((kernel_parts, grad_cols))
+    grad_rows = exchange(grad_cols).transpose(1, 0, 2, 3).reshape(grad_out.shape)
+
+    kernel_parts = [by_column(part) for part in kernel_parts]
+    half_at = my_index // half * half_len
+    half_cos = lax.dynamic_slice_in_dim(cosine_outer, half_at, half_len, 1)
+    half_sin = lax.dynamic_slice_in_dim(sine_outer, half_at, half_len, 1)
+    first = (my_index % half * half_cols).astype(jnp.int32).reshape(1)
+    nothing = jnp.zeros_like(filter_w)
+    paired_w = jnp.concatenate(
+        (
+            jnp.concatenate((filter_w, nothing), axis=1),
+            jnp.concatenate((nothing, filter_w), axis=1),
+        ),
+        axis=0,
+    )
+    paired_decay = jnp.concatenate((decay, decay))[None]
+    weight_shape, slope_shape = (PAIR * order, PAIR * lanes), (8, PAIR * lanes)
+    weight, slope = call(
+        functools.partial(filter_kernel, inner_len, inv_total, inv_root),
+        half_cols // PAIR,
+        [pl.BlockSpec(memory_space=pltpu.SMEM), whole(half_cos), whole(half_sin),
+         block(kernel_parts[0], 0, PAIR), block(kernel_parts[1], 0, PAIR), block(hidden, 1, 1),
+         whole(paired_w), whole(paired_decay)],
+        [whole(f32(weight_shape)), whole(f32(slope_shape))],
+        [f32(weight_shape), f32(slope_shape)],
+        outer_flops,
+        table_bytes // 2 + 3 * column_bytes,
+        first, half_cos, half_sin, *kernel_parts, hidden, paired_w, paired_decay,
+    )
+    weight = weight[:order, :lanes] + weight[order:, lanes:]
+    slope = jnp.sum(slope[:, :lanes] + slope[:, lanes:], axis=0, keepdims=True)
+    both = jnp.concatenate((weight, -slope * inv_root), axis=0)
+    step = 1
+    while step < devices:
+        pairs = [(source, source ^ step) for source in range(devices)]
+        both = both + lax.ppermute(both, "outer", pairs)
+        step *= 2
+    return (grad_rows, both[:order], both[order])
+
+
 def solution(mesh):
     placed = (
         P(("grp", "outer"), None, None),

time: 1130 us -> 890 us (0.79)
  waiting for transfers between devices: 640 us -> 282 us
  blocking collectives: 38.8 us -> 302 us
  matrix products: 261 us -> 0 us
  Pallas kernels: 0 us -> 105 us
  other arithmetic: 3.88 us -> 91.6 us
  local copies, waits for them, and re-layouts: 147 us -> 71.3 us
    all_to_all x9 -> x5, waiting for transfers between devices: 640 us -> 233 us  [exchange(): lax.all_to_all(values, 'outer', split_axis=0, concat_axis=0, axis_index_g...]
    all_to_all x0 -> x4, blocking collectives: none -> 302 us  [exchange(): lax.all_to_all(values, 'outer', split_axis=0, concat_axis=0, axis_index_g...]
    dot_general x20 -> x0, matrix products: 261 us -> none  [the longest x6 141 us: outer_section(): jnp.dot(matrix, flattened, preferred_element_type=jnp.float32)]
    pallas_call x0 -> x5, Pallas kernels: none -> 105 us  [call(): pl.pallas_call(kernel, grid=(grid,), in_specs=in_specs, out_specs=out_spe...]
    sin x0 -> x2, other arithmetic: none -> 63.6 us  [twiddle(): return (jnp.cos(angles)[:, :, None], jnp.sin(angles)[:, :, None])]
    ppermute x0 -> x5, waiting for transfers between devices: none -> 49.9 us  [shards(): both = both + lax.ppermute(both, 'outer', pairs)]
    convert_element_type x9 -> x2, local copies, waits for them, and re-layouts: 51.6 us -> 9.41 us  [twiddle(): angles = product.astype(jnp.float32) * (2.0 * math.pi / seq_len)]
    psum x1 -> x0, blocking collectives: 38.8 us -> none  [shards(): grad_filter_w, grad_decay = lax.psum((weight_part, decay_part), 'outer')]
  transfers between devices with their start and end apart: 9 -> 10, of which waited for: 9 -> 9; matrix products, arithmetic and copies ran while one was open for 18% -> 16% of each run, Pallas kernels for 0% -> 4%
where the time goes in v1:
time: 890 us; the launch traced here: 888 us
  blocking collectives  302 us (34%)
  waiting for transfers between devices  282 us (32%)
  Pallas kernels  105 us (12%)
  other arithmetic  91.6 us (10%)
  local copies, waits for them, and re-layouts  71.3 us (8%)
  starting transfers between devices  35.3 us (4%)
    all_to_all x4, blocking collectives, exchange(): lax.all_to_all(values, 'outer', split_axis=0, concat_axis=0, axis_index_g...  302 us
    all_to_all x5, waiting for transfers between devices, exchange(): lax.all_to_all(values, 'outer', split_axis=0, concat_axis=0, axis_index_g...  233 us
    pallas_call x5, Pallas kernels, call(): pl.pallas_call(kernel, grid=(grid,), in_specs=in_specs, out_specs=out_spe...  105 us
    sin x2, other arithmetic, twiddle(): return (jnp.cos(angles)[:, :, None], jnp.sin(angles)[:, :, None])  63.6 us
    ppermute x5, waiting for transfers between devices, shards(): both = both + lax.ppermute(both, 'outer', pairs)  49.9 us
    all_to_all x5, starting transfers between devices, exchange(): lax.all_to_all(values, 'outer', split_axis=0, concat_axis=0, axis_index_g...  23.7 us
    convert_element_type x2, other arithmetic, cos_sin(): jnp.sin(angles).astype(jnp.bfloat16)  22.7 us
  transfers between devices with their start and end apart: 10, of which 9 were waited for; matrix products, arithmetic and copies ran while one was open for 16% of the time, Pallas kernels for 4%

profile of v1, /device:TPU:0, one launch (start us, length us, event | category | flops | bytes accessed | tf_op | source)
XLA Modules:
  0.0 888.5 jit_solution(3641558666639172845)
XLA Ops:
  0.6 6.9 copy.42
  7.5 7.6 all-to-all-start
  15.2 0.1 fusion.17
  15.3 0.0 copy-start.7
  15.3 4.7 copy.39
  20.0 0.0 copy-done.7
  20.0 3.2 copy.40
  23.2 5.0 reshape.260
  28.3 1.4 copy.54
  29.7 2.3 pad_maximum_fusion
  32.0 17.7 %sine_convert_fusion = (bf16[1024,1024]{1,0:T(8,128)(2,1)}, bf16[1024,1024]{1,0:T(8,128)(2,1)}) fusion(), kind=kLoop, calls=%fused_computation.12 | loop fusion | flops 16777216 | bytes 4194304 | tf_op jit(solution)/shard_map/convert_element_type | solution.py:20
  49.7 31.9 %multiply_sine_fusion = (f32[16,1024,1]{2,1,0:T(8,128)}, f32[16,1024,1]{2,1,0:T(8,128)}) fusion(f32[16,1024,1]{2,1,0:T(8,128)} %copy.39), kind=kLoop, calls=%fused_computation | loop fusion | flops 16384 | bytes 196608 | tf_op jit(solution)/shard_map/sin | solution.py:26
  81.6 27.4 %all-to-all-done.x_ref = bf16[32,16,32,128]{3,2,1,0:T(8,128)(2,1)} async-done(((bf16[32,16,32,128]{3,2,1,0:T(8,128)(2,1)}), bf16[32,16,32,128]{3,2,1,0:T(8,128)(2,1)}, u32[]{:S(2)}, u32[]{:S(2)}) %all-to-all-start) | async-done | bytes 4194336 | tf_op jit(solution)/shard_map/all_to_all | solution.py:276
  108.9 17.3 %shard_map.85 = (bf16[16,1024,128]{2,1,0:T(8,128)(2,1)}, bf16[16,1024,128]{2,1,0:T(8,128)(2,1)}) custom-call(bf16[1024,1024]{1,0:T(8,128)(2,1)} %get-tuple-element.48.cos_ref, bf16[1024,1024]{1,0:T(8,128)(2,1)} %get-tuple-element.47.sin_ref, f32[16,1024,1]{2,1,0:T(8,128)} %get-tuple-element.44.tc_ref, f32[16,1024,1]{2,1,0:T(8,128)} %get-tuple-element.43.ts_ref, ...), custom_call_target="tpu_custom_call" | custom-call | flops 8589934592 | bytes 33554432 | tf_op jit(solution)/shard_map/pallas_call | solution.py:140
  126.3 6.8 copy.43
  133.1 4.2 all-to-all-start.1
  137.3 6.9 copy.44
  144.2 86.9 %all-to-all-done.1.fr_ref = bf16[32,32,16,128]{3,2,1,0:T(8,128)(2,1)} async-done(((bf16[32,32,16,128]{3,2,1,0:T(8,128)(2,1)}), bf16[32,32,16,128]{3,2,1,0:T(8,128)(2,1)}, u32[]{:S(2)}, u32[]{:S(2)}) %all-to-all-start.1) | async-done | bytes 4194336 | tf_op jit(solution)/shard_map/all_to_all | solution.py:276
  231.2 3.9 all-to-all-start.2
  235.1 0.1 fusion.15
  235.2 4.7 copy.38
  239.9 5.0 sine_convert_fusion.1
  244.8 31.8 %multiply_sine_fusion.1 = (f32[32,512,1]{2,1,0:T(8,128)}, f32[32,512,1]{2,1,0:T(8,128)}) fusion(f32[32,512,1]{2,1,0:T(8,128)} %copy.38), kind=kLoop, calls=%fused_computation.2 | loop fusion | flops 16384 | bytes 196608 | tf_op jit(solution)/shard_map/sin | solution.py:26
  276.6 52.3 %all-to-all-done.2.fi_ref = bf16[32,32,16,128]{3,2,1,0:T(8,128)(2,1)} async-done(((bf16[32,32,16,128]{3,2,1,0:T(8,128)(2,1)}), bf16[32,32,16,128]{3,2,1,0:T(8,128)(2,1)}, u32[]{:S(2)}, u32[]{:S(2)}) %all-to-all-start.2) | async-done | bytes 4194336 | tf_op jit(solution)/shard_map/all_to_all | solution.py:276
  328.9 26.9 %shard_map.86 = (bf16[32,32,16,128]{3,2,1,0:T(8,128)(2,1)}, bf16[32,32,16,128]{3,2,1,0:T(8,128)(2,1)}) custom-call(bf16[512,512]{1,0:T(8,128)(2,1)} %get-tuple-element.50.cos_ref, bf16[512,512]{1,0:T(8,128)(2,1)} %get-tuple-element.49.sin_ref, f32[32,512,1]{2,1,0:T(8,128)} %get-tuple-element.46.tc_ref, f32[32,512,1]{2,1,0:T(8,128)} %get-tuple-element.45.ts_ref, ...), custom_call_target="tpu_custom_call" | custom-call | flops 17179869184 | bytes 41943040 | tf_op jit(solution)/shard_map/pallas_call | solution.py:140
  355.8 26.9 %shard_map.87 = (bf16[16,32,32,128]{3,2,1,0:T(8,128)(2,1)}, bf16[16,32,32,128]{3,2,1,0:T(8,128)(2,1)}) custom-call(bf16[512,512]{1,0:T(8,128)(2,1)} %get-tuple-element.50.cos_ref, bf16[512,512]{1,0:T(8,128)(2,1)} %get-tuple-element.49.sin_ref, f32[32,512,1]{2,1,0:T(8,128)} %get-tuple-element.46.tc_ref, f32[32,512,1]{2,1,0:T(8,128)} %get-tuple-element.45.ts_ref, ...), custom_call_target="tpu_custom_call" | custom-call | flops 17179869184 | bytes 41943040 | tf_op jit(solution)/shard_map/pallas_call | solution.py:140
  382.7 54.7 %all_to_all.45 = bf16[16,32,32,128]{3,2,1,0:T(8,128)(2,1)} all-to-all(bf16[16,32,32,128]{3,2,1,0:T(8,128)(2,1)} %get-tuple-element.27), channel_id=1, replica_groups={{0,1,2,3,4,5,6,7,8,9,10,11,12,13,14,15},{16,17,18,19,20,21,22,23,24,25,..., dimensions={0} | all-to-all | bytes 8388608 | tf_op jit(solution)/shard_map/all_to_all | solution.py:276
  437.4 53.5 %all_to_all.46 = bf16[16,32,32,128]{3,2,1,0:T(8,128)(2,1)} all-to-all(bf16[16,32,32,128]{3,2,1,0:T(8,128)(2,1)S(1)} %copy-done.6), channel_id=1, replica_groups={{0,1,2,3,4,5,6,7,8,9,10,11,12,13,14,15},{16,17,18,19,20,21,22,23,24,25,..., dimensions={0} | all-to-all | bytes 8388608 | tf_op jit(solution)/shard_map/all_to_all | solution.py:276
  490.9 96.2 %all_to_all.47 = bf16[32,32,16,128]{3,2,1,0:T(8,128)(2,1)} all-to-all(bf16[32,32,16,128]{3,2,1,0:T(8,128)(2,1)S(1)} %copy-done.5), channel_id=1, replica_groups=mesh['grp'=1,'outer'=32] {'outer'}, dimensions={0} | all-to-all | bytes 8388608 | tf_op jit(solution)/shard_map/all_to_all | solution.py:276
  587.1 0.0 copy-done.4
  587.1 97.2 %all_to_all.48 = bf16[32,32,16,128]{3,2,1,0:T(8,128)(2,1)} all-to-all(bf16[32,32,16,128]{3,2,1,0:T(8,128)(2,1)S(1)} %copy-done.4), channel_id=1, replica_groups=mesh['grp'=1,'outer'=32] {'outer'}, dimensions={0} | all-to-all | bytes 8388608 | tf_op jit(solution)/shard_map/all_to_all | solution.py:276
  684.3 4.1 all-to-all-start.8
  688.4 5.4 copy.46
  693.9 3.1 copy.45
  697.0 14.0 %shard_map.88 = bf16[16,1024,128]{2,1,0:T(8,128)(2,1)} custom-call(bf16[1024,1024]{1,0:T(8,128)(2,1)} %get-tuple-element.48.cos_ref, bf16[1024,1024]{1,0:T(8,128)(2,1)} %get-tuple-element.47.sin_ref, bf16[16,1024,128]{2,1,0:T(8,128)(2,1)} %bitcast.45, bf16[16,1024,128]{2,1,0:T(8,128)(2,1)} %bitcast.44), custom_call_target="tpu_custom_call" | custom-call | flops 8589934592 | bytes 16777216 | tf_op jit(solution)/shard_map/pallas_call | solution.py:140
  710.9 5.5 copy.53
  716.4 65.9 %all-to-all-done.8.hidden_ref = bf16[32,16,32,128]{3,2,1,0:T(8,128)(2,1)} async-done(((bf16[32,16,32,128]{3,2,1,0:T(8,128)(2,1)}), bf16[32,16,32,128]{3,2,1,0:T(8,128)(2,1)}, u32[]{:S(2)}, u32[]{:S(2)}) %all-to-all-start.8) | async-done | bytes 4194336 | tf_op jit(solution)/shard_map/all_to_all | solution.py:276
  782.3 3.9 all-to-all-start.7
  786.2 0.0 copy-done.9
  786.2 0.0 copy-start
  786.2 0.6 pad_maximum_fusion.2
  786.8 0.6 fusion.18.w_ref
  787.4 2.3 constant_dynamic-slice_fusion.sin_ref
  789.8 0.0 copy-done.3
  789.8 1.1 constant_dynamic-slice_fusion.1.cos_ref
  790.8 3.6 copy.48
  794.4 3.6 copy.49
  798.0 20.4 %shard_map.89 = (f32[128,256]{1,0:T(8,128)}, f32[8,256]{1,0:T(8,128)}) custom-call(s32[1]{0:T(128)} %bitcast.15.first_ref, bf16[1024,512]{1,0:T(8,128)(2,1)} %constant_dynamic-slice_fusion.1.cos_ref, bf16[1024,512]{1,0:T(8,128)(2,1)} %constant_dynamic-slice_fusion.sin_ref, bf16[32,512,128]{2,1,0:T(8,128)(2,1)} %bitcast.42, bf16[32,512,128]{2,1,0:T(8,128)(2,1)} %bitcast.43, ...), custom_call_target="tpu_custom_call" | custom-call | flops 8589934592 | bytes 14680064 | tf_op jit(solution)/shard_map/pallas_call | solution.py:140
  818.4 0.7 add_reduce_fusion
  819.2 0.8 slice_add_fusion
  819.9 0.2 collective-permute-start
  820.2 1.0 collective-permute-done
  821.2 1.7 collective-permute-start.1
  822.9 2.3 collective-permute-done.1
  825.2 5.9 collective-permute-start.2
  831.1 4.1 collective-permute-done.2
  835.2 0.0 collective-permute-start.3
  835.2 20.9 %collective-permute-done.3 = f32[65,128]{1,0:T(8,128)S(1)} collective-permute-done((f32[65,128]{1,0:T(8,128)S(1)}, f32[65,128]{1,0:T(8,128)S(1)}, u32[]{:S(2)}, u32[]{:S(2)}) %collective-permute-start.3) | collective-permute-done | bytes 33312 | tf_op jit(solution)/shard_map/ppermute | solution.py:393
  856.1 3.8 collective-permute-start.4
  860.0 21.5 %collective-permute-done.4 = f32[65,128]{1,0:T(8,128)S(1)} collective-permute-done((f32[65,128]{1,0:T(8,128)S(1)}, f32[65,128]{1,0:T(8,128)S(1)}, u32[]{:S(2)}, u32[]{:S(2)}) %collective-permute-start.4) | collective-permute-done | bytes 33312 | tf_op jit(solution)/shard_map/ppermute | solution.py:393
  881.5 0.6 slice.24
  882.1 0.5 slice_bitcast_fusion
  882.6 0.0 all-to-all-done.7
  882.6 5.8 copy.50
  (23 shorter events, 0.1 us)
Async XLA Ops:
  7.5 101.4 %all-to-all-start = ((bf16[32,16,32,128]{3,2,1,0:T(8,128)(2,1)}), bf16[32,16,32,128]{3,2,1,0:T(8,128)(2,1)}, u32[]{:S(2)}, u32[]{:S(2)}) async-start(bf16[32,16,32,128]{3,2,1,0:T(8,128)(2,1)} %bitcast.36), calls=%async_computation | async-start | bytes 8388608 | tf_op jit(solution)/shard_map/all_to_all | solution.py:276
  15.3 4.8 copy-start.7
  133.1 98.0 %all-to-all-start.1 = ((bf16[32,32,16,128]{3,2,1,0:T(8,128)(2,1)}), bf16[32,32,16,128]{3,2,1,0:T(8,128)(2,1)}, u32[]{:S(2)}, u32[]{:S(2)}) async-start(bf16[32,32,16,128]{3,2,1,0:T(8,128)(2,1)} %bitcast.38), calls=%async_computation.1 | async-start | bytes 8388608 | tf_op jit(solution)/shard_map/all_to_all | solution.py:276
  231.2 97.8 %all-to-all-start.2 = ((bf16[32,32,16,128]{3,2,1,0:T(8,128)(2,1)}), bf16[32,32,16,128]{3,2,1,0:T(8,128)(2,1)}, u32[]{:S(2)}, u32[]{:S(2)}) async-start(bf16[32,32,16,128]{3,2,1,0:T(8,128)(2,1)} %bitcast.37), calls=%async_computation.2 | async-start | bytes 8388608 | tf_op jit(solution)/shard_map/all_to_all | solution.py:276
  382.7 54.7 %copy-start.6 = (bf16[16,32,32,128]{3,2,1,0:T(8,128)(2,1)S(1)}, bf16[16,32,32,128]{3,2,1,0:T(8,128)(2,1)}, u32[]{:S(2)}) copy-start(bf16[16,32,32,128]{3,2,1,0:T(8,128)(2,1)} %get-tuple-element.28) | copy-start | bytes 12582916
  437.4 53.5 %copy-start.5 = (bf16[32,32,16,128]{3,2,1,0:T(8,128)(2,1)S(1)}, bf16[32,32,16,128]{3,2,1,0:T(8,128)(2,1)}, u32[]{:S(2)}) copy-start(bf16[32,32,16,128]{3,2,1,0:T(8,128)(2,1)} %get-tuple-element.30) | copy-start | bytes 12582916
  490.9 96.2 %copy-start.4 = (bf16[32,32,16,128]{3,2,1,0:T(8,128)(2,1)S(1)}, bf16[32,32,16,128]{3,2,1,0:T(8,128)(2,1)}, u32[]{:S(2)}) copy-start(bf16[32,32,16,128]{3,2,1,0:T(8,128)(2,1)} %get-tuple-element.29) | copy-start | bytes 12582916
  684.3 97.9 %all-to-all-start.8 = ((bf16[32,16,32,128]{3,2,1,0:T(8,128)(2,1)}), bf16[32,16,32,128]{3,2,1,0:T(8,128)(2,1)}, u32[]{:S(2)}, u32[]{:S(2)}) async-start(bf16[32,16,32,128]{3,2,1,0:T(8,128)(2,1)} %pad_maximum_fusion), calls=%async_computation.8 | async-start | bytes 8388608 | tf_op jit(solution)/shard_map/all_to_all | solution.py:276
  688.4 5.4 copy-start.2
  716.4 69.8 %copy-start.9 = (f32[128]{0:T(128)S(1)}, f32[128]{0:T(128)}, u32[]{:S(2)}) copy-start(f32[128]{0:T(128)} %param.11) | copy-start | bytes 1540
  716.4 70.4 %copy-start.8 = (bf16[64,128]{1,0:T(8,128)(2,1)S(1)}, bf16[64,128]{1,0:T(8,128)(2,1)}, u32[]{:S(2)}) copy-start(bf16[64,128]{1,0:T(8,128)(2,1)} %param.10) | copy-start | bytes 49156
  716.4 73.4 %copy-start.3 = (bf16[1024,1024]{1,0:T(8,128)(2,1)S(1)}, bf16[1024,1024]{1,0:T(8,128)(2,1)}, u32[]{:S(2)}) copy-start(bf16[1024,1024]{1,0:T(8,128)(2,1)} %get-tuple-element.48.cos_ref) | copy-start | bytes 6291460
  782.3 100.4 %all-to-all-start.7 = ((bf16[32,32,16,128]{3,1,2,0:T(8,128)(2,1)}), bf16[32,32,16,128]{3,1,2,0:T(8,128)(2,1)}, u32[]{:S(2)}, u32[]{:S(2)}) async-start(bf16[32,32,16,128]{3,1,2,0:T(8,128)(2,1)} %bitcast.33), calls=%async_computation.7 | async-start | bytes 8388608 | tf_op jit(solution)/shard_map/all_to_all | solution.py:276
  786.2 4.6 copy-start
  790.8 3.6 copy-start.1
  819.9 1.3 collective-permute-start
  821.2 4.0 collective-permute-start.1
  825.2 10.0 %collective-permute-start.2 = (f32[65,128]{1,0:T(8,128)S(1)}, f32[65,128]{1,0:T(8,128)S(1)}, u32[]{:S(2)}, u32[]{:S(2)}) collective-permute-start(f32[65,128]{1,0:T(8,128)S(1)} %add.129), channel_id=1, source_target_pairs={{0,4},{1,5},{2,6},{3,7},{4,0},{5,1},{6,2},{7,3},{8,12},{9,13},{10,... | collective-permute-start | bytes 99848 | tf_op jit(solution)/shard_map/ppermute | solution.py:393
  835.2 21.0 %collective-permute-start.3 = (f32[65,128]{1,0:T(8,128)S(1)}, f32[65,128]{1,0:T(8,128)S(1)}, u32[]{:S(2)}, u32[]{:S(2)}) collective-permute-start(f32[65,128]{1,0:T(8,128)S(1)} %add.130), channel_id=1, source_target_pairs={{0,8},{1,9},{2,10},{3,11},{4,12},{5,13},{6,14},{7,15},{8,0},{9,1},... | collective-permute-start | bytes 99848 | tf_op jit(solution)/shard_map/ppermute | solution.py:393
  856.1 25.4 %collective-permute-start.4 = (f32[65,128]{1,0:T(8,128)S(1)}, f32[65,128]{1,0:T(8,128)S(1)}, u32[]{:S(2)}, u32[]{:S(2)}) collective-permute-start(f32[65,128]{1,0:T(8,128)S(1)} %add.131), channel_id=1, source_target_pairs={{0,16},{1,17},{2,18},{3,19},{4,20},{5,21},{6,22},{7,23},{8,24},{9,... | collective-permute-start | bytes 99848 | tf_op jit(solution)/shard_map/ppermute | solution.py:393

commit v2 on v1

--- a/solution.py
+++ b/solution.py
@@ -128,6 +128,13 @@
     return (grad_rows, grad_filter_w, grad_decay)
 
 
+def turns(first_numbers, second_numbers, seq_len):
+    product = first_numbers[:, None] * second_numbers[None, :] % seq_len
+    angles = product.astype(jnp.float32) * (2.0 * math.pi / seq_len)
+    cosine, sine = lax.optimization_barrier((jnp.cos(angles), jnp.sin(angles)))
+    return (cosine[:, :, None], sine[:, :, None])
+
+
 def dot(matrix, values):
     return jnp.dot(matrix, values, preferred_element_type=jnp.float32)
 
@@ -288,11 +295,20 @@
     hidden = filter_hidden.reshape(rows_dev, half, half_cols // PAIR, PAIR * order)
     hidden = hidden.transpose(1, 2, 0, 3)
     hidden = jnp.concatenate((hidden, hidden), axis=0)
-    hidden, columns = lax.optimization_barrier((hidden, columns))
-    hidden = exchange(hidden)
-
+    middle = hidden.shape[1] // 2
     my_cols = my_index * cols_dev + jnp.arange(cols_dev, dtype=jnp.int32)
-    twist_cos, twist_sin = twiddle(my_cols, jnp.arange(outer_len, dtype=jnp.int32), seq_len)
+    twist_cos, twist_sin = turns(my_cols, jnp.arange(outer_len, dtype=jnp.int32), seq_len)
+    my_freq = my_index * freq_dev + jnp.arange(freq_dev, dtype=jnp.int32)
+    back_cos, back_sin = turns(my_freq, jnp.arange(inner_len, dtype=jnp.int32), seq_len)
+    tables = (cosine_outer, sine_outer, cosine_inner, sine_inner)
+    twists = (twist_cos, twist_sin, back_cos, back_sin)
+    early_hidden, columns, tables, twists = lax.optimization_barrier(
+        (hidden[:, :middle], columns, tables, twists)
+    )
+    cosine_outer, sine_outer, cosine_inner, sine_inner = tables
+    twist_cos, twist_sin, back_cos, back_sin = twists
+    early_hidden = exchange(early_hidden)
+
     table_bytes = 4 * outer_len * outer_len
     column_bytes = 2 * outer_len * cols_dev * lanes
     turn_bytes = 8 * 128 * outer_len * cols_dev
@@ -310,12 +326,16 @@
         table_bytes + 3 * column_bytes + turn_bytes,
         cosine_outer, sine_outer, twist_cos, twist_sin, columns,
     )
-    freq_real, freq_imag = [
-        exchange(part.reshape(cols_dev, devices, freq_dev, lanes).transpose(1, 2, 0, 3))
+    shifted = [
+        part.reshape(cols_dev, devices, freq_dev, lanes).transpose(1, 2, 0, 3)
         for part in shifted
     ]
-    my_freq = my_index * freq_dev + jnp.arange(freq_dev, dtype=jnp.int32)
-    back_cos, back_sin = twiddle(my_freq, jnp.arange(inner_len, dtype=jnp.int32), seq_len)
+    early_hidden, shifted = lax.optimization_barrier((early_hidden, shifted))
+    freq_real, freq_imag = [exchange(part) for part in shifted]
+    late_hidden, freq_real, freq_imag = lax.optimization_barrier(
+        (hidden[:, middle:], freq_real, freq_imag)
+    )
+    late_hidden = exchange(late_hidden)
 
     def turned_of(spectrum, freq_real, freq_imag, pieces):
         shape = (pieces, freq_dev, inner_len // pieces, lanes)
@@ -340,8 +360,11 @@
         ((freq_real, freq_imag), input_turned)
     )
     kernel_turned = turned_of(input_spec, freq_real, freq_imag, half)
-    input_parts = [by_column(exchange(part)) for part in input_turned]
+    late_hidden, input_turned = lax.optimization_barrier((late_hidden, input_turned))
+    input_parts = [exchange(part) for part in input_turned]
+    kernel_turned, input_parts = lax.optimization_barrier((kernel_turned, input_parts))
     kernel_parts = [exchange(part, groups) for part in kernel_turned]
+    input_parts = [by_column(part) for part in input_parts]
 
     grad_cols = call(
         functools.partial(outer_inverse_kernel, inv_total),
@@ -362,6 +385,7 @@
     half_cos = lax.dynamic_slice_in_dim(cosine_outer, half_at, half_len, 1)
     half_sin = lax.dynamic_slice_in_dim(sine_outer, half_at, half_len, 1)
     first = (my_index % half * half_cols).astype(jnp.int32).reshape(1)
+    hidden = jnp.concatenate((early_hidden, late_hidden), axis=1)
     nothing = jnp.zeros_like(filter_w)
     paired_w = jnp.concatenate(
         (

time: 890 us -> 836 us (0.939)
  other arithmetic: 91.6 us -> 32.4 us
  waiting for transfers between devices: 282 us -> 223 us
  blocking collectives: 302 us -> 347 us
  local copies, waits for them, and re-layouts: 71.3 us -> 83.5 us
    sin x2, other arithmetic: 63.6 us -> 0.68 us  [turns(): cosine, sine = lax.optimization_barrier((jnp.cos(angles), jnp.sin(angles)))]
    all_to_all x5 -> x6, waiting for transfers between devices: 233 us -> 181 us  [exchange(): lax.all_to_all(values, 'outer', split_axis=0, concat_axis=0, axis_index_g...]
    all_to_all x4, blocking collectives: 302 us -> 347 us  [exchange(): lax.all_to_all(values, 'outer', split_axis=0, concat_axis=0, axis_index_g...]
    optimization_barrier x0 -> x4, local copies, waits for them, and re-layouts: none -> 18.5 us  [shards(): lax.optimization_barrier((hidden[:, :middle], columns, tables, twists))]
    convert_element_type x2 -> x0, local copies, waits for them, and re-layouts: 9.41 us -> none  [twiddle(): angles = product.astype(jnp.float32) * (2.0 * math.pi / seq_len)]
    all_to_all x5 -> x6, starting transfers between devices: 23.7 us -> 30.3 us  [exchange(): lax.all_to_all(values, 'outer', split_axis=0, concat_axis=0, axis_index_g...]
  transfers between devices with their start and end apart: 10 -> 11, of which waited for: 9 -> 10; matrix products, arithmetic and copies ran while one was open for 16% -> 12% of each run, Pallas kernels for 4% -> 13%
where the time goes in v2:
time: 836 us; the launch traced here: 834 us
  blocking collectives  347 us (42%)
  waiting for transfers between devices  223 us (27%)
  Pallas kernels  105 us (13%)
  local copies, waits for them, and re-layouts  83.5 us (10%)
  starting transfers between devices  41.6 us (5%)
  other arithmetic  32.4 us (4%)
    all_to_all x4, blocking collectives, exchange(): lax.all_to_all(values, 'outer', split_axis=0, concat_axis=0, axis_index_g...  347 us
    all_to_all x6, waiting for transfers between devices, exchange(): lax.all_to_all(values, 'outer', split_axis=0, concat_axis=0, axis_index_g...  181 us
    pallas_call x5, Pallas kernels, call(): pl.pallas_call(kernel, grid=(grid,), in_specs=in_specs, out_specs=out_spe...  105 us
    ppermute x5, waiting for transfers between devices, shards(): both = both + lax.ppermute(both, 'outer', pairs)  42.9 us
    all_to_all x6, starting transfers between devices, exchange(): lax.all_to_all(values, 'outer', split_axis=0, concat_axis=0, axis_index_g...  30.3 us
    convert_element_type x2, other arithmetic, cos_sin(): jnp.sin(angles).astype(jnp.bfloat16)  22.7 us
    transpose x4, local copies, waits for them, and re-layouts, by_column(): return part.transpose(2, 0, 1, 3).reshape(part.shape[2], -1, lanes)  19.9 us
    optimization_barrier x4, local copies, waits for them, and re-layouts, shards(): lax.optimization_barrier((hidden[:, :middle], columns, tables, twists))  18.5 us
  transfers between devices with their start and end apart: 11, of which 10 were waited for; matrix products, arithmetic and copies ran while one was open for 12% of the time, Pallas kernels for 13%

profile of v2, /device:TPU:0, one launch (start us, length us, event | category | flops | bytes accessed | tf_op | source)
XLA Modules:
  0.0 834.3 jit_solution(2140149641024654875)
XLA Ops:
  0.6 6.9 copy.51
  7.5 7.4 all-to-all-start
  15.0 0.3 fusion.30
  15.3 0.3 fusion.28
  15.7 0.0 copy-done.3
  15.7 3.1 copy.49
  18.8 5.0 reshape.62
  23.9 1.4 copy.69
  25.2 4.9 sine_convert_fusion.1
  30.2 2.2 pad_maximum_fusion.1
  32.4 17.7 %sine_convert_fusion = (bf16[1024,1024]{1,0:T(8,128)(2,1)}, bf16[1024,1024]{1,0:T(8,128)(2,1)}) fusion(), kind=kLoop, calls=%fused_computation.10 | loop fusion | flops 16777216 | bytes 4194304 | tf_op jit(solution)/shard_map/convert_element_type | solution.py:20
  50.1 58.7 %all-to-all-done.x_ref = bf16[32,16,32,128]{3,2,1,0:T(8,128)(2,1)} async-done(((bf16[32,16,32,128]{3,2,1,0:T(8,128)(2,1)}), bf16[32,16,32,128]{3,2,1,0:T(8,128)(2,1)}, u32[]{:S(2)}, u32[]{:S(2)}) %all-to-all-start) | async-done | bytes 4194336 | tf_op jit(solution)/shard_map/all_to_all | solution.py:283
  108.8 4.1 all-to-all-start.1
  113.0 4.6 copy.52.tc_ref
  117.6 4.5 copy.53.ts_ref
  122.2 17.3 %shard_map.85 = (bf16[16,1024,128]{2,1,0:T(8,128)(2,1)}, bf16[16,1024,128]{2,1,0:T(8,128)(2,1)}) custom-call(bf16[1024,1024]{1,0:T(8,128)(2,1)} %get-tuple-element.54.cos_ref, bf16[1024,1024]{1,0:T(8,128)(2,1)} %get-tuple-element.55.sin_ref, f32[16,1024,1]{2,1,0:T(8,128)} %copy.52.tc_ref, f32[16,1024,1]{2,1,0:T(8,128)} %copy.53.ts_ref, ...), custom_call_target="tpu_custom_call" | custom-call | flops 8589934592 | bytes 33554432 | tf_op jit(solution)/shard_map/pallas_call | solution.py:147
  139.5 7.0 copy.55
  146.5 0.0 copy-done.2
  146.5 4.7 copy.54
  151.2 10.5 %all-to-all-done.1 = bf16[32,8,32,128]{3,2,1,0:T(8,128)(2,1)S(1)} async-done(((bf16[32,8,32,128]{3,2,1,0:T(8,128)(2,1)}), bf16[32,8,32,128]{3,2,1,0:T(8,128)(2,1)S(1)}, u32[]{:S(2)}, u32[]{:S(2)}) %all-to-all-start.1) | async-done | bytes 2097184 | tf_op jit(solution)/shard_map/all_to_all | solution.py:283
  161.8 97.7 %all_to_all.50.fr_ref = bf16[32,32,16,128]{3,2,1,0:T(8,128)(2,1)} all-to-all(bf16[32,32,16,128]{3,2,1,0:T(8,128)(2,1)} %bitcast.42), channel_id=1, replica_groups=mesh['grp'=1,'outer'=32] {'outer'}, dimensions={0} | all-to-all | bytes 8388608 | tf_op jit(solution)/shard_map/all_to_all | solution.py:283
  259.5 0.0 copy-done.1
  259.5 97.3 %all_to_all.51.fi_ref = bf16[32,32,16,128]{3,2,1,0:T(8,128)(2,1)} all-to-all(bf16[32,32,16,128]{3,2,1,0:T(8,128)(2,1)S(1)} %bitcast.41), channel_id=1, replica_groups=mesh['grp'=1,'outer'=32] {'outer'}, dimensions={0} | all-to-all | bytes 8388608 | tf_op jit(solution)/shard_map/all_to_all | solution.py:283
  356.7 3.8 all-to-all-start.4
  360.6 4.7 copy.58.tc_ref
  365.3 4.6 copy.59.ts_ref
  369.9 26.9 %shard_map.86 = (bf16[32,32,16,128]{3,2,1,0:T(8,128)(2,1)}, bf16[32,32,16,128]{3,2,1,0:T(8,128)(2,1)}) custom-call(bf16[512,512]{1,0:T(8,128)(2,1)} %get-tuple-element.49.cos_ref, bf16[512,512]{1,0:T(8,128)(2,1)} %get-tuple-element.50.sin_ref, f32[32,512,1]{2,1,0:T(8,128)} %copy.58.tc_ref, f32[32,512,1]{2,1,0:T(8,128)} %copy.59.ts_ref, ...), custom_call_target="tpu_custom_call" | custom-call | flops 17179869184 | bytes 41943040 | tf_op jit(solution)/shard_map/pallas_call | solution.py:147
  396.8 12.6 %all-to-all-done.4 = bf16[32,8,32,128]{3,2,1,0:T(8,128)(2,1)} async-done(((bf16[32,8,32,128]{3,2,1,0:T(8,128)(2,1)}), bf16[32,8,32,128]{3,2,1,0:T(8,128)(2,1)}, u32[]{:S(2)}, u32[]{:S(2)}) %all-to-all-start.4) | async-done | bytes 2097184 | tf_op jit(solution)/shard_map/all_to_all | solution.py:283
  409.5 97.8 %all_to_all.52 = bf16[32,32,16,128]{3,2,1,0:T(8,128)(2,1)} all-to-all(bf16[32,32,16,128]{3,2,1,0:T(8,128)(2,1)} %get-tuple-element.74), channel_id=1, replica_groups=mesh['grp'=1,'outer'=32] {'outer'}, dimensions={0} | all-to-all | bytes 8388608 | tf_op jit(solution)/shard_map/all_to_all | solution.py:283
  507.2 4.1 all-to-all-start.6
  511.3 26.9 %shard_map.87 = (bf16[16,32,32,128]{3,2,1,0:T(8,128)(2,1)}, bf16[16,32,32,128]{3,2,1,0:T(8,128)(2,1)}) custom-call(bf16[512,512]{1,0:T(8,128)(2,1)} %get-tuple-element.49.cos_ref, bf16[512,512]{1,0:T(8,128)(2,1)} %get-tuple-element.50.sin_ref, f32[32,512,1]{2,1,0:T(8,128)} %copy.58.tc_ref, f32[32,512,1]{2,1,0:T(8,128)} %copy.59.ts_ref, ...), custom_call_target="tpu_custom_call" | custom-call | flops 17179869184 | bytes 41943040 | tf_op jit(solution)/shard_map/pallas_call | solution.py:147
  538.2 66.9 %all-to-all-done.6 = bf16[32,32,16,128]{3,2,1,0:T(8,128)(2,1)} async-done(((bf16[32,32,16,128]{3,2,1,0:T(8,128)(2,1)}), bf16[32,32,16,128]{3,2,1,0:T(8,128)(2,1)}, u32[]{:S(2)}, u32[]{:S(2)}) %all-to-all-start.6) | async-done | bytes 4194336 | tf_op jit(solution)/shard_map/all_to_all | solution.py:283
  605.1 54.4 %all_to_all.53 = bf16[16,32,32,128]{3,2,1,0:T(8,128)(2,1)} all-to-all(bf16[16,32,32,128]{3,2,1,0:T(8,128)(2,1)} %get-tuple-element.76), channel_id=1, replica_groups={{0,1,2,3,4,5,6,7,8,9,10,11,12,13,14,15},{16,17,18,19,20,21,22,23,24,25,..., dimensions={0} | all-to-all | bytes 8388608 | tf_op jit(solution)/shard_map/all_to_all | solution.py:283
  659.6 4.5 all-to-all-start.8
  664.1 5.3 copy.60
  669.4 5.2 copy.61
  674.6 13.9 %shard_map.88 = bf16[16,1024,128]{2,1,0:T(8,128)(2,1)} custom-call(bf16[1024,1024]{1,0:T(8,128)(2,1)} %get-tuple-element.54.cos_ref, bf16[1024,1024]{1,0:T(8,128)(2,1)} %get-tuple-element.55.sin_ref, bf16[16,1024,128]{2,1,0:T(8,128)(2,1)} %bitcast.46, bf16[16,1024,128]{2,1,0:T(8,128)(2,1)} %bitcast.47), custom_call_target="tpu_custom_call" | custom-call | flops 8589934592 | bytes 16777216 | tf_op jit(solution)/shard_map/pallas_call | solution.py:147
  688.6 5.5 copy.68
  694.0 31.7 %all-to-all-done.8 = bf16[16,32,32,128]{3,2,1,0:T(8,128)(2,1)} async-done(((bf16[16,32,32,128]{3,2,1,0:T(8,128)(2,1)}), bf16[16,32,32,128]{3,2,1,0:T(8,128)(2,1)}, u32[]{:S(2)}, u32[]{:S(2)}) %all-to-all-start.8) | async-done | bytes 4194336 | tf_op jit(solution)/shard_map/all_to_all | solution.py:283
  725.7 6.3 all-to-all-start.9
  732.1 0.6 pad_maximum_fusion.3
  732.7 0.6 fusion.21.w_ref
  733.3 2.3 constant_dynamic-slice_fusion.sin_ref
  735.6 2.3 constant_dynamic-slice_fusion.1.cos_ref
  737.9 4.0 pad_maximum_fusion.hidden_ref
  741.9 3.6 copy.63
  745.5 5.8 copy.64
  751.3 20.4 %shard_map.89 = (f32[128,256]{1,0:T(8,128)}, f32[8,256]{1,0:T(8,128)}) custom-call(s32[1]{0:T(128)} %bitcast.19.first_ref, bf16[1024,512]{1,0:T(8,128)(2,1)} %constant_dynamic-slice_fusion.1.cos_ref, bf16[1024,512]{1,0:T(8,128)(2,1)} %constant_dynamic-slice_fusion.sin_ref, bf16[32,512,128]{2,1,0:T(8,128)(2,1)} %bitcast.44, bf16[32,512,128]{2,1,0:T(8,128)(2,1)} %bitcast.45, ...), custom_call_target="tpu_custom_call" | custom-call | flops 8589934592 | bytes 14680064 | tf_op jit(solution)/shard_map/pallas_call | solution.py:147
  771.7 0.7 add_reduce_fusion
  772.4 0.8 slice_add_fusion
  773.2 0.1 collective-permute-start
  773.3 1.2 collective-permute-done
  774.5 1.4 collective-permute-start.1
  775.9 6.5 collective-permute-done.1
  782.4 0.0 collective-permute-start.2
  782.4 4.3 collective-permute-done.2
  786.8 5.6 collective-permute-start.3
  792.3 9.1 %collective-permute-done.3 = f32[65,128]{1,0:T(8,128)S(1)} collective-permute-done((f32[65,128]{1,0:T(8,128)S(1)}, f32[65,128]{1,0:T(8,128)S(1)}, u32[]{:S(2)}, u32[]{:S(2)}) %collective-permute-start.3) | collective-permute-done | bytes 33312 | tf_op jit(solution)/shard_map/ppermute | solution.py:417
  801.4 4.2 collective-permute-start.4
  805.6 21.8 %collective-permute-done.4 = f32[65,128]{1,0:T(8,128)S(1)} collective-permute-done((f32[65,128]{1,0:T(8,128)S(1)}, f32[65,128]{1,0:T(8,128)S(1)}, u32[]{:S(2)}, u32[]{:S(2)}) %collective-permute-start.4) | collective-permute-done | bytes 33312 | tf_op jit(solution)/shard_map/ppermute | solution.py:417
  827.3 0.6 slice.34
  828.0 0.5 slice_bitcast_fusion
  828.5 0.0 all-to-all-done.9
  828.5 5.8 copy.65
  (18 shorter events, 0.1 us)
Async XLA Ops:
  7.5 8.2 copy-start.3
  7.5 101.3 %all-to-all-start = ((bf16[32,16,32,128]{3,2,1,0:T(8,128)(2,1)}), bf16[32,16,32,128]{3,2,1,0:T(8,128)(2,1)}, u32[]{:S(2)}, u32[]{:S(2)}) async-start(bf16[32,16,32,128]{3,2,1,0:T(8,128)(2,1)} %bitcast.39), calls=%async_computation | async-start | bytes 8388608 | tf_op jit(solution)/shard_map/all_to_all | solution.py:283
  108.8 52.9 %all-to-all-start.1 = ((bf16[32,8,32,128]{3,2,1,0:T(8,128)(2,1)}), bf16[32,8,32,128]{3,2,1,0:T(8,128)(2,1)S(1)}, u32[]{:S(2)}, u32[]{:S(2)}) async-start(bf16[32,8,32,128]{3,2,1,0:T(8,128)(2,1)} %get-tuple-element.53), calls=%async_computation.1 | async-start | bytes 4194304 | tf_op jit(solution)/shard_map/all_to_all | solution.py:283
  139.5 7.0 copy-start.2
  161.8 97.7 %copy-start.1 = (bf16[16,1024,128]{2,0,1:T(8,128)(2,1)S(1)}, bf16[16,1024,128]{2,0,1:T(8,128)(2,1)}, u32[]{:S(2)}) copy-start(bf16[16,1024,128]{2,0,1:T(8,128)(2,1)} %copy.55) | copy-start | bytes 12582916
  356.7 52.7 %all-to-all-start.4 = ((bf16[32,8,32,128]{3,2,1,0:T(8,128)(2,1)}), bf16[32,8,32,128]{3,2,1,0:T(8,128)(2,1)}, u32[]{:S(2)}, u32[]{:S(2)}) async-start(bf16[32,8,32,128]{3,2,1,0:T(8,128)(2,1)} %get-tuple-element.71), calls=%async_computation.4 | async-start | bytes 4194304 | tf_op jit(solution)/shard_map/all_to_all | solution.py:283
  507.2 97.9 %all-to-all-start.6 = ((bf16[32,32,16,128]{3,2,1,0:T(8,128)(2,1)}), bf16[32,32,16,128]{3,2,1,0:T(8,128)(2,1)}, u32[]{:S(2)}, u32[]{:S(2)}) async-start(bf16[32,32,16,128]{3,2,1,0:T(8,128)(2,1)} %get-tuple-element.75), calls=%async_computation.6 | async-start | bytes 8388608 | tf_op jit(solution)/shard_map/all_to_all | solution.py:283
  659.6 66.2 %all-to-all-start.8 = ((bf16[16,32,32,128]{3,2,1,0:T(8,128)(2,1)}), bf16[16,32,32,128]{3,2,1,0:T(8,128)(2,1)}, u32[]{:S(2)}, u32[]{:S(2)}) async-start(bf16[16,32,32,128]{3,2,1,0:T(8,128)(2,1)} %get-tuple-element.77), calls=%async_computation.8 | async-start | bytes 8388608 | tf_op jit(solution)/shard_map/all_to_all | solution.py:283
  725.7 6.3 copy-start.5
  725.7 6.9 copy-start.4
  725.7 102.7 %all-to-all-start.9 = ((bf16[32,32,16,128]{3,1,2,0:T(8,128)(2,1)}), bf16[32,32,16,128]{3,1,2,0:T(8,128)(2,1)}, u32[]{:S(2)}, u32[]{:S(2)}) async-start(bf16[32,32,16,128]{3,1,2,0:T(8,128)(2,1)} %bitcast.37), calls=%async_computation.9 | async-start | bytes 8388608 | tf_op jit(solution)/shard_map/all_to_all | solution.py:283
  737.9 4.0 copy-start
  773.2 1.3 collective-permute-start
  774.5 7.9 collective-permute-start.1
  782.4 4.3 collective-permute-start.2
  786.8 14.6 %collective-permute-start.3 = (f32[65,128]{1,0:T(8,128)S(1)}, f32[65,128]{1,0:T(8,128)S(1)}, u32[]{:S(2)}, u32[]{:S(2)}) collective-permute-start(f32[65,128]{1,0:T(8,128)S(1)} %add.96), channel_id=1, source_target_pairs={{0,8},{1,9},{2,10},{3,11},{4,12},{5,13},{6,14},{7,15},{8,0},{9,1},... | collective-permute-start | bytes 99848 | tf_op jit(solution)/shard_map/ppermute | solution.py:417
  801.4 25.9 %collective-permute-start.4 = (f32[65,128]{1,0:T(8,128)S(1)}, f32[65,128]{1,0:T(8,128)S(1)}, u32[]{:S(2)}, u32[]{:S(2)}) collective-permute-start(f32[65,128]{1,0:T(8,128)S(1)} %add.97), channel_id=1, source_target_pairs={{0,16},{1,17},{2,18},{3,19},{4,20},{5,21},{6,22},{7,23},{8,24},{9,... | collective-permute-start | bytes 99848 | tf_op jit(solution)/shard_map/ppermute | solution.py:417
